TPU v7x, 1024 devices: a whole 8x8x8 slice. The times are simulated.
1024 devices in a mesh: dp: 32 (over x, y_hi), mp: 32 (over z, y_lo, core).
Axes of the slice: x: 8, y: 8 (y_hi: 4, y_lo: 2; y = y_hi * 2 + y_lo), z: 8, core: 2. Of those that a mesh axis runs over, the one named last changes fastest.
Arguments:
- stream: bfloat16 [262144, 1152], P(('dp', 'mp')), may hold values from -6 to 6
- query_key_value: bfloat16 [262144, 3456], P(('dp', 'mp')), may hold values from -9 to 9
- lengths: int32 [1024, 3], P(('dp', 'mp')), may hold values from 1 to 160, 256 in all within a row
- out_weight: bfloat16 [1152, 1152], P('mp', 'dp'), may hold values from -0.1875 to 0.1875
- text_embed: bfloat16 [3072, 1152], P(('dp', 'mp')), may hold values from -6 to 6
- logit_scale: float32 [1], replicated, may hold values from 5 to 20
- logit_bias: float32 [1], replicated, may hold values from -6 to -3
Outputs:
- stream_out: bfloat16 [262144, 1152], P(('dp', 'mp'))
- image_grad: float32 [3072, 1152], P(('dp', 'mp'))
- text_grad: float32 [3072, 1152], P(('dp', 'mp'))
Inputs may be any that keep to these rules, and one draw needn't show every extreme that they name: `lengths`: the 3 counts of each pack sum to 256; the largest of each pack is exactly 160.
All inputs are finite; a program needn't handle non-finite values.
Results may differ from a plain program's by a relative error of at most 0.0034.
Values may be sent and summed in bfloat16 or wider, within the bound.
A program may use at most 32 MiB of HBM per device.

v0:
```python
import math

import jax
import jax.numpy as jnp
from jax import lax
from jax.sharding import PartitionSpec as P

HEADS = 16


def from_behind(block, axis, distance):
    devices = range(lax.axis_size(axis))
    route = [((i - distance) % len(devices), i) for i in devices]
    return lax.ppermute(block, axis, route)


def attend_pack(packed, counts, head_count):
    row_count = packed.shape[0]
    model_width = packed.shape[1] // 3
    head_size = model_width // head_count
    queries = packed[:, :model_width].reshape(row_count, head_count, head_size)
    key_rows = packed[:, model_width : 2 * model_width].reshape(row_count, head_count, head_size)
    value_rows = packed[:, 2 * model_width :].reshape(row_count, head_count, head_size)
    boundary = jnp.cumsum(counts, dtype=jnp.int32)
    places = jnp.arange(row_count, dtype=jnp.int32)
    segment = jnp.sum((places[:, None] >= boundary[None, :-1]).astype(jnp.int32), axis=1)
    same_image = segment[:, None] == segment[None, :]
    scores = jnp.einsum(
        "qhd,khd->hqk", queries, key_rows, preferred_element_type=jnp.float32
    ) / math.sqrt(head_size)
    scores = jnp.where(same_image[None], scores, jnp.float32(-1e30))
    peaks = jnp.max(scores, axis=2, keepdims=True)
    raised = jnp.exp(scores - peaks)
    attention = (raised / jnp.sum(raised, axis=2, keepdims=True)).astype(jnp.bfloat16)
    context = jnp.einsum("hqk,khd->qhd", attention, value_rows, preferred_element_type=jnp.float32)
    context = context.reshape(row_count, model_width).astype(jnp.bfloat16)
    image_slots = jnp.arange(counts.shape[0], dtype=jnp.int32)
    member = (segment[:, None] == image_slots[None, :]).astype(jnp.bfloat16)
    return (context, member)


def unit_rows(values):
    squares = jnp.sum(values * values, axis=1, keepdims=True)
    return values / jnp.sqrt(squares + 1e-06)


def coefficients(row_images, texts, image_ids, text_ids, scale, offset):
    logits = scale * jnp.dot(row_images, texts.T, precision=lax.Precision.HIGHEST) + offset
    labels = jnp.where(image_ids[:, None] == text_ids[None, :], jnp.float32(1.0), jnp.float32(-1.0))
    return -labels * jax.nn.sigmoid(-labels * logits)


def per_device(stream, query_key_value, lengths, out_weight, text_embed, logit_scale, logit_bias):
    counts = lengths[0]
    context, member = attend_pack(query_key_value, counts, HEADS)
    weight_block = lax.all_gather(out_weight, "mp", axis=0, tiled=True)
    product = jnp.dot(
        context,
        lax.all_gather(weight_block, "dp", axis=1, tiled=True),
        preferred_element_type=jnp.float32,
    )
    mixed = (product + stream.astype(jnp.float32)).astype(jnp.bfloat16)
    pooled = jnp.dot(member.T, mixed, preferred_element_type=jnp.float32)
    pooled = pooled / counts.astype(jnp.float32)[:, None]
    image_unit = unit_rows(pooled)
    text_unit = unit_rows(text_embed.astype(jnp.float32))
    row_images = lax.all_gather(image_unit, "mp", axis=0, tiled=True)
    scale = logit_scale[0]
    offset = logit_bias[0]
    dp_index = lax.axis_index("dp")
    mp_index = lax.axis_index("mp")
    cycle_length = lax.axis_size("dp")
    column_length = lax.axis_size("mp")
    images_here = image_unit.shape[0]
    image_ids = dp_index * column_length * images_here + jnp.arange(
        row_images.shape[0], dtype=jnp.int32
    )
    own_slots = jnp.arange(images_here, dtype=jnp.int32)
    carried = jnp.stack([text_unit, jnp.zeros(text_unit.shape, jnp.float32)])

    def turn(number, state):
        travelling, image_part = state
        anchor = (dp_index - number) % cycle_length
        text_ids = (anchor * column_length + mp_index) * images_here + own_slots
        coef = coefficients(row_images, travelling[0], image_ids, text_ids, scale, offset)
        image_part = image_part + scale * jnp.dot(
            coef, travelling[0], precision=lax.Precision.HIGHEST
        )
        text_part = travelling[1] + scale * jnp.dot(
            coef.T, row_images, precision=lax.Precision.HIGHEST
        )
        moved = from_behind(jnp.stack([travelling[0], text_part]), "dp", 1)
        return (moved, image_part)

    start_state = (carried, jnp.zeros(row_images.shape, jnp.float32))
    carried, image_part = lax.fori_loop(0, cycle_length, turn, start_state)
    text_grad = carried[1]
    image_grad = lax.psum_scatter(image_part, "mp", scatter_dimension=0, tiled=True)
    return (mixed, image_grad, text_grad)


def solution(mesh):
    in_specs = (
        P(("dp", "mp"), None),
        P(("dp", "mp"), None),
        P(("dp", "mp"), None),
        P("mp", "dp"),
        P(("dp", "mp"), None),
        P(),
        P(),
    )
    out_specs = (P(("dp", "mp"), None), P(("dp", "mp"), None), P(("dp", "mp"), None))
    return jax.shard_map(
        per_device, mesh=mesh, in_specs=in_specs, out_specs=out_specs, check_vma=False
    )
```

profile of v0, /device:TPU:1, one launch (start us, length us, event | category | flops | bytes accessed | tf_op | source)
XLA Modules:
  0.0 851.2 jit_solution(1316218946313979874)
XLA Ops:
  7.2 49.8 %all-gather = bf16[32,36,36]{2,1,0:T(8,128)(2,1)S(1)} all-gather(bf16[1,36,36]{2,1,0:T(8,128)(2,1)} %bitcast.67), channel_id=1, replica_groups=mesh['dp'=32,'mp'=32] {'mp'}, dimensions={0}, use_global_device_ids=true | all-gather | bytes 85536 | tf_op jit(solution)/shard_map/all_gather | solution.py:56
  69.9 79.5 %all-gather.5.cloned.1.call-done = bf16[32,36,1152]{2,1,0:T(8,128)(2,1)} async-done(((bf16[1,36,1152]{2,1,0:T(8,128)(2,1)}), bf16[32,36,1152]{2,1,0:T(8,128)(2,1)}) %all-gather.5.cloned.1.call-update) | async-done | bytes 2654224 | tf_op jit(solution)/shard_map/all_gather | solution.py:59
  156.1 38.9 %all-gather.2 = f32[32,3,1152]{2,1,0:T(4,128)S(1)} all-gather(f32[1,3,1152]{2,1,0:T(4,128)S(1)} %divide_bitcast_fusion), channel_id=1, replica_groups=mesh['dp'=32,'mp'=32] {'mp'}, dimensions={0}, use_global_device_ids=true | all-gather | bytes 456192 | tf_op jit(solution)/shard_map/all_gather | solution.py:67
  195.2 379.9 %while.18 = (s32[]{:T(128)}, f32[2,3,1152]{2,1,0:T(4,128)S(1)}, f32[96,1152]{1,0:T(8,128)S(1)}, f32[]{:T(128)}, s32[]{:T(128)}, /*index=5*/s32[]{:T(128)}, f32[9...) while((s32[]{:T(128)}, f32[2,3,1152]{2,1,0:T(4,128)S(1)}, ...), condition=%wide.region_7.8_spmd.clone, body=%wide.region_6.7_spmd.clone.sunk | while | flops 12292533 | bytes 2088952 | solution.py:96
  213.2 5.6 collective-permute-done
  236.8 5.6 collective-permute-done
  248.7 5.9 collective-permute-done
  260.8 5.6 collective-permute-done
  284.4 5.6 collective-permute-done
  308.1 5.6 collective-permute-done
  331.7 6.2 collective-permute-done
  344.1 5.7 collective-permute-done
  367.8 5.6 collective-permute-done
  391.5 5.6 collective-permute-done
  415.1 5.6 collective-permute-done
  438.8 5.6 collective-permute-done
  462.4 6.0 collective-permute-done
  474.6 5.6 collective-permute-done
  486.4 5.9 collective-permute-done
  498.6 5.6 collective-permute-done
  510.4 5.6 collective-permute-done
  534.0 5.6 collective-permute-done
  569.5 5.6 collective-permute-done
  576.5 266.3 %all-reduce.4.cloned.1.call-done = f32[96,1152]{1,0:T(8,128)} async-done(((f32[96,1152]{1,0:T(8,128)}), f32[96,1152]{1,0:T(8,128)}) %all-reduce.4.cloned.1.call-update) | async-done | bytes 442384
  (340 shorter events, 290.1 us)
Async XLA Ops:
  7.2 142.2 %all-gather.5.cloned.1.call-start = ((), (), s32[]{:S(2)}) async-start(), calls=%async_computation | async-start | bytes 3041280 | tf_op jit(solution)/shard_map/all_gather | solution.py:59
  57.9 784.9 %all-reduce.4.cloned.1.call-start = ((), (), s32[]{:S(2)}) async-start(), calls=%async_computation.1 | async-start | bytes 884736
  198.1 8.9 %collective-permute-start = (f32[2,3,1152]{2,1,0:T(4,128)S(1)}, f32[2,3,1152]{2,1,0:T(4,128)S(1)}, u32[]{:S(2)}, u32[]{:S(2)}) collective-permute-start(f32[2,3,1152]{2,1,0:T(4,128)S(1)} %pad_maximum_fusion.2), channel_id=1, source_target_pairs={{992,0},{0,32},{32,64},{64,96},{96,128},{128,160},{160,192},{192,2... | collective-permute-start | bytes 82952 | tf_op jit(solution)/shard_map/while/body/eval_jaxpr/ppermute | solution.py:14
  209.9 8.9 %collective-permute-start = (f32[2,3,1152]{2,1,0:T(4,128)S(1)}, f32[2,3,1152]{2,1,0:T(4,128)S(1)}, u32[]{:S(2)}, u32[]{:S(2)}) collective-permute-start(f32[2,3,1152]{2,1,0:T(4,128)S(1)} %pad_maximum_fusion.2), channel_id=1, source_target_pairs={{992,0},{0,32},{32,64},{64,96},{96,128},{128,160},{160,192},{192,2... | collective-permute-start | bytes 82952 | tf_op jit(solution)/shard_map/while/body/eval_jaxpr/ppermute | solution.py:14
  221.7 8.9 %collective-permute-start = (f32[2,3,1152]{2,1,0:T(4,128)S(1)}, f32[2,3,1152]{2,1,0:T(4,128)S(1)}, u32[]{:S(2)}, u32[]{:S(2)}) collective-permute-start(f32[2,3,1152]{2,1,0:T(4,128)S(1)} %pad_maximum_fusion.2), channel_id=1, source_target_pairs={{992,0},{0,32},{32,64},{64,96},{96,128},{128,160},{160,192},{192,2... | collective-permute-start | bytes 82952 | tf_op jit(solution)/shard_map/while/body/eval_jaxpr/ppermute | solution.py:14
  233.6 8.9 %collective-permute-start = (f32[2,3,1152]{2,1,0:T(4,128)S(1)}, f32[2,3,1152]{2,1,0:T(4,128)S(1)}, u32[]{:S(2)}, u32[]{:S(2)}) collective-permute-start(f32[2,3,1152]{2,1,0:T(4,128)S(1)} %pad_maximum_fusion.2), channel_id=1, source_target_pairs={{992,0},{0,32},{32,64},{64,96},{96,128},{128,160},{160,192},{192,2... | collective-permute-start | bytes 82952 | tf_op jit(solution)/shard_map/while/body/eval_jaxpr/ppermute | solution.py:14
  245.4 9.2 %collective-permute-start = (f32[2,3,1152]{2,1,0:T(4,128)S(1)}, f32[2,3,1152]{2,1,0:T(4,128)S(1)}, u32[]{:S(2)}, u32[]{:S(2)}) collective-permute-start(f32[2,3,1152]{2,1,0:T(4,128)S(1)} %pad_maximum_fusion.2), channel_id=1, source_target_pairs={{992,0},{0,32},{32,64},{64,96},{96,128},{128,160},{160,192},{192,2... | collective-permute-start | bytes 82952 | tf_op jit(solution)/shard_map/while/body/eval_jaxpr/ppermute | solution.py:14
  257.5 8.9 %collective-permute-start = (f32[2,3,1152]{2,1,0:T(4,128)S(1)}, f32[2,3,1152]{2,1,0:T(4,128)S(1)}, u32[]{:S(2)}, u32[]{:S(2)}) collective-permute-start(f32[2,3,1152]{2,1,0:T(4,128)S(1)} %pad_maximum_fusion.2), channel_id=1, source_target_pairs={{992,0},{0,32},{32,64},{64,96},{96,128},{128,160},{160,192},{192,2... | collective-permute-start | bytes 82952 | tf_op jit(solution)/shard_map/while/body/eval_jaxpr/ppermute | solution.py:14
  269.3 8.9 %collective-permute-start = (f32[2,3,1152]{2,1,0:T(4,128)S(1)}, f32[2,3,1152]{2,1,0:T(4,128)S(1)}, u32[]{:S(2)}, u32[]{:S(2)}) collective-permute-start(f32[2,3,1152]{2,1,0:T(4,128)S(1)} %pad_maximum_fusion.2), channel_id=1, source_target_pairs={{992,0},{0,32},{32,64},{64,96},{96,128},{128,160},{160,192},{192,2... | collective-permute-start | bytes 82952 | tf_op jit(solution)/shard_map/while/body/eval_jaxpr/ppermute | solution.py:14
  281.1 8.9 %collective-permute-start = (f32[2,3,1152]{2,1,0:T(4,128)S(1)}, f32[2,3,1152]{2,1,0:T(4,128)S(1)}, u32[]{:S(2)}, u32[]{:S(2)}) collective-permute-start(f32[2,3,1152]{2,1,0:T(4,128)S(1)} %pad_maximum_fusion.2), channel_id=1, source_target_pairs={{992,0},{0,32},{32,64},{64,96},{96,128},{128,160},{160,192},{192,2... | collective-permute-start | bytes 82952 | tf_op jit(solution)/shard_map/while/body/eval_jaxpr/ppermute | solution.py:14
  292.9 8.9 %collective-permute-start = (f32[2,3,1152]{2,1,0:T(4,128)S(1)}, f32[2,3,1152]{2,1,0:T(4,128)S(1)}, u32[]{:S(2)}, u32[]{:S(2)}) collective-permute-start(f32[2,3,1152]{2,1,0:T(4,128)S(1)} %pad_maximum_fusion.2), channel_id=1, source_target_pairs={{992,0},{0,32},{32,64},{64,96},{96,128},{128,160},{160,192},{192,2... | collective-permute-start | bytes 82952 | tf_op jit(solution)/shard_map/while/body/eval_jaxpr/ppermute | solution.py:14
  304.8 8.9 %collective-permute-start = (f32[2,3,1152]{2,1,0:T(4,128)S(1)}, f32[2,3,1152]{2,1,0:T(4,128)S(1)}, u32[]{:S(2)}, u32[]{:S(2)}) collective-permute-start(f32[2,3,1152]{2,1,0:T(4,128)S(1)} %pad_maximum_fusion.2), channel_id=1, source_target_pairs={{992,0},{0,32},{32,64},{64,96},{96,128},{128,160},{160,192},{192,2... | collective-permute-start | bytes 82952 | tf_op jit(solution)/shard_map/while/body/eval_jaxpr/ppermute | solution.py:14
  316.6 8.9 %collective-permute-start = (f32[2,3,1152]{2,1,0:T(4,128)S(1)}, f32[2,3,1152]{2,1,0:T(4,128)S(1)}, u32[]{:S(2)}, u32[]{:S(2)}) collective-permute-start(f32[2,3,1152]{2,1,0:T(4,128)S(1)} %pad_maximum_fusion.2), channel_id=1, source_target_pairs={{992,0},{0,32},{32,64},{64,96},{96,128},{128,160},{160,192},{192,2... | collective-permute-start | bytes 82952 | tf_op jit(solution)/shard_map/while/body/eval_jaxpr/ppermute | solution.py:14
  328.4 9.5 %collective-permute-start = (f32[2,3,1152]{2,1,0:T(4,128)S(1)}, f32[2,3,1152]{2,1,0:T(4,128)S(1)}, u32[]{:S(2)}, u32[]{:S(2)}) collective-permute-start(f32[2,3,1152]{2,1,0:T(4,128)S(1)} %pad_maximum_fusion.2), channel_id=1, source_target_pairs={{992,0},{0,32},{32,64},{64,96},{96,128},{128,160},{160,192},{192,2... | collective-permute-start | bytes 82952 | tf_op jit(solution)/shard_map/while/body/eval_jaxpr/ppermute | solution.py:14
  340.8 9.0 %collective-permute-start = (f32[2,3,1152]{2,1,0:T(4,128)S(1)}, f32[2,3,1152]{2,1,0:T(4,128)S(1)}, u32[]{:S(2)}, u32[]{:S(2)}) collective-permute-start(f32[2,3,1152]{2,1,0:T(4,128)S(1)} %pad_maximum_fusion.2), channel_id=1, source_target_pairs={{992,0},{0,32},{32,64},{64,96},{96,128},{128,160},{160,192},{192,2... | collective-permute-start | bytes 82952 | tf_op jit(solution)/shard_map/while/body/eval_jaxpr/ppermute | solution.py:14
  352.7 8.9 %collective-permute-start = (f32[2,3,1152]{2,1,0:T(4,128)S(1)}, f32[2,3,1152]{2,1,0:T(4,128)S(1)}, u32[]{:S(2)}, u32[]{:S(2)}) collective-permute-start(f32[2,3,1152]{2,1,0:T(4,128)S(1)} %pad_maximum_fusion.2), channel_id=1, source_target_pairs={{992,0},{0,32},{32,64},{64,96},{96,128},{128,160},{160,192},{192,2... | collective-permute-start | bytes 82952 | tf_op jit(solution)/shard_map/while/body/eval_jaxpr/ppermute | solution.py:14
  364.6 8.9 %collective-permute-start = (f32[2,3,1152]{2,1,0:T(4,128)S(1)}, f32[2,3,1152]{2,1,0:T(4,128)S(1)}, u32[]{:S(2)}, u32[]{:S(2)}) collective-permute-start(f32[2,3,1152]{2,1,0:T(4,128)S(1)} %pad_maximum_fusion.2), channel_id=1, source_target_pairs={{992,0},{0,32},{32,64},{64,96},{96,128},{128,160},{160,192},{192,2... | collective-permute-start | bytes 82952 | tf_op jit(solution)/shard_map/while/body/eval_jaxpr/ppermute | solution.py:14
  376.4 8.9 %collective-permute-start = (f32[2,3,1152]{2,1,0:T(4,128)S(1)}, f32[2,3,1152]{2,1,0:T(4,128)S(1)}, u32[]{:S(2)}, u32[]{:S(2)}) collective-permute-start(f32[2,3,1152]{2,1,0:T(4,128)S(1)} %pad_maximum_fusion.2), channel_id=1, source_target_pairs={{992,0},{0,32},{32,64},{64,96},{96,128},{128,160},{160,192},{192,2... | collective-permute-start | bytes 82952 | tf_op jit(solution)/shard_map/while/body/eval_jaxpr/ppermute | solution.py:14
  388.2 8.9 %collective-permute-start = (f32[2,3,1152]{2,1,0:T(4,128)S(1)}, f32[2,3,1152]{2,1,0:T(4,128)S(1)}, u32[]{:S(2)}, u32[]{:S(2)}) collective-permute-start(f32[2,3,1152]{2,1,0:T(4,128)S(1)} %pad_maximum_fusion.2), channel_id=1, source_target_pairs={{992,0},{0,32},{32,64},{64,96},{96,128},{128,160},{160,192},{192,2... | collective-permute-start | bytes 82952 | tf_op jit(solution)/shard_map/while/body/eval_jaxpr/ppermute | solution.py:14
  400.0 8.9 %collective-permute-start = (f32[2,3,1152]{2,1,0:T(4,128)S(1)}, f32[2,3,1152]{2,1,0:T(4,128)S(1)}, u32[]{:S(2)}, u32[]{:S(2)}) collective-permute-start(f32[2,3,1152]{2,1,0:T(4,128)S(1)} %pad_maximum_fusion.2), channel_id=1, source_target_pairs={{992,0},{0,32},{32,64},{64,96},{96,128},{128,160},{160,192},{192,2... | collective-permute-start | bytes 82952 | tf_op jit(solution)/shard_map/while/body/eval_jaxpr/ppermute | solution.py:14
  411.8 8.9 %collective-permute-start = (f32[2,3,1152]{2,1,0:T(4,128)S(1)}, f32[2,3,1152]{2,1,0:T(4,128)S(1)}, u32[]{:S(2)}, u32[]{:S(2)}) collective-permute-start(f32[2,3,1152]{2,1,0:T(4,128)S(1)} %pad_maximum_fusion.2), channel_id=1, source_target_pairs={{992,0},{0,32},{32,64},{64,96},{96,128},{128,160},{160,192},{192,2... | collective-permute-start | bytes 82952 | tf_op jit(solution)/shard_map/while/body/eval_jaxpr/ppermute | solution.py:14
  459.1 9.3 %collective-permute-start = (f32[2,3,1152]{2,1,0:T(4,128)S(1)}, f32[2,3,1152]{2,1,0:T(4,128)S(1)}, u32[]{:S(2)}, u32[]{:S(2)}) collective-permute-start(f32[2,3,1152]{2,1,0:T(4,128)S(1)} %pad_maximum_fusion.2), channel_id=1, source_target_pairs={{992,0},{0,32},{32,64},{64,96},{96,128},{128,160},{160,192},{192,2... | collective-permute-start | bytes 82952 | tf_op jit(solution)/shard_map/while/body/eval_jaxpr/ppermute | solution.py:14
  471.3 8.9 %collective-permute-start = (f32[2,3,1152]{2,1,0:T(4,128)S(1)}, f32[2,3,1152]{2,1,0:T(4,128)S(1)}, u32[]{:S(2)}, u32[]{:S(2)}) collective-permute-start(f32[2,3,1152]{2,1,0:T(4,128)S(1)} %pad_maximum_fusion.2), channel_id=1, source_target_pairs={{992,0},{0,32},{32,64},{64,96},{96,128},{128,160},{160,192},{192,2... | collective-permute-start | bytes 82952 | tf_op jit(solution)/shard_map/while/body/eval_jaxpr/ppermute | solution.py:14
  483.2 9.2 %collective-permute-start = (f32[2,3,1152]{2,1,0:T(4,128)S(1)}, f32[2,3,1152]{2,1,0:T(4,128)S(1)}, u32[]{:S(2)}, u32[]{:S(2)}) collective-permute-start(f32[2,3,1152]{2,1,0:T(4,128)S(1)} %pad_maximum_fusion.2), channel_id=1, source_target_pairs={{992,0},{0,32},{32,64},{64,96},{96,128},{128,160},{160,192},{192,2... | collective-permute-start | bytes 82952 | tf_op jit(solution)/shard_map/while/body/eval_jaxpr/ppermute | solution.py:14
  (14 other events, 147.3 us)
Sparse Core Ops, SparseCore 0:
  58.1 91.2 all-gather.4
  576.0 266.7 all-reduce.3
where the time goes:
time: 854 us; the launch traced here: 851 us
  waiting for transfers between devices  525 us (61%)
  matrix products  142 us (17%)
  blocking collectives  88.7 us (10%)
  starting transfers between devices  64.6 us (8%)
  between operations  14.9 us (2%)
  local copies, waits for them, and re-layouts  11.9 us (1%)
    unnamed x3, waiting for transfers between devices  266 us
    ppermute x32, waiting for transfers between devices, from_behind(): return lax.ppermute(block, axis, route)  179 us
    all_gather x1, waiting for transfers between devices, per_device(): lax.all_gather(weight_block, 'dp', axis=1, tiled=True)  79.5 us
    ppermute x32, starting transfers between devices, from_behind(): return lax.ppermute(block, axis, route)  64.6 us
    dot_general x32, matrix products, coefficients(): jnp.dot(row_images, texts.T, precision=lax.Precision.HIGHEST)  57.1 us
    all_gather x1, blocking collectives, per_device(): weight_block = lax.all_gather(out_weight, 'mp', axis=0, tiled=True)  49.8 us
    dot_general x32, matrix products, turn(): jnp.dot(coef, travelling[0], precision=lax.Precision.HIGHEST)  43 us
    all_gather x1, blocking collectives, per_device(): row_images = lax.all_gather(image_unit, 'mp', axis=0, tiled=True)  38.9 us
  transfers between devices with their start and end apart: 34, of which 34 were waited for; matrix products, arithmetic and copies ran while one was open for 6% of the time, Pallas kernels for 0%

commit v1 on v0

v1 whole, which is shorter than its diff:
```python
import functools
import math

import jax
import jax.numpy as jnp
from jax import lax
from jax.experimental import pallas as pl
from jax.experimental.pallas import tpu as pltpu
from jax.sharding import PartitionSpec as P

MESH = pl.DeviceIdType.MESH
HEADS = 16
HEAD = 72
SLAB = 80
ROWS = 256
D = 1152
BLK = 36
HIGHEST = lax.Precision.HIGHEST
STEPS = ((1, 0, 0, 1), (-1, 0, 0, -1), (0, 1, 0, 2), (0, -1, 0, -2), (0, 0, 1, 3), (0, 0, -1, -3))
FAR = ((0, 2, 0, 0, 256), (0, -2, 0, 256, 256), (1, 0, 1, 512, 384), (-1, 0, -1, 896, 256))


def place():
    dp, mp = lax.axis_index("dp"), lax.axis_index("mp")
    return dp // 4, 2 * (dp % 4) + (mp // 2) % 2, mp // 4, mp % 2


def device(x, y, z, c):
    return (x * 4 + y // 2, z * 4 + (y % 2) * 2 + c)


def step_from(x, y, z, c, sx, sy, sz):
    return device((x + sx + 8) % 8, (y + sy + 8) % 8, (z + sz + 8) % 8, c)


def send(src, dst, send_sem, recv_sem, to):
    copy = pltpu.make_async_remote_copy(
        src_ref=src, dst_ref=dst, send_sem=send_sem, recv_sem=recv_sem, device_id=to, device_id_type=MESH
    )
    copy.start()
    return copy


def await_bytes(ref, sem):
    pltpu.make_async_copy(ref, ref, sem).wait()


def shift_lanes(value, amount):
    amount = amount % 128
    return value if amount == 0 else pltpu.roll(value, amount, 1)


def split(value):
    high = value.astype(jnp.bfloat16)
    low = (value - high.astype(jnp.float32)).astype(jnp.bfloat16)
    return high, low


def dot32(a, b, dims):
    return lax.dot_general(a, b, (dims, ((), ())), preferred_element_type=jnp.float32)


def kernel(
    lengths, scale_ref, bias_ref, weight, text, qkv_hbm, stream_hbm,
    out, image_grad, text_grad,
    qkv, stream, raw, rows72, packed, arrived, slabs, context,
    texts, images, table_i, table_t,
    part_i, part_x, sent_i, got_i, sent_t, got_t,
    local_sem, raw_s, raw_r, one_s, one_r, two_s, two_r, fwd_s, fwd_r,
    text_s, text_r, img_s, img_r, imf_s, imf_r, mix_s, mix_r, gi_s, gi_r, gt_s, gt_r,
):
    x, y, z, c = place()
    dp, mp = lax.axis_index("dp"), lax.axis_index("mp")
    yh, yl = y // 2, y % 2
    pair = z * 2 + yl
    sibling = device(x, y, z, 1 - c)
    mine = (x + 2 * y + 3 * z) % 8

    load_qkv = pltpu.make_async_copy(qkv_hbm, qkv, local_sem.at[0])
    load_qkv.start()
    load_stream = pltpu.make_async_copy(stream_hbm, stream, local_sem.at[1])
    load_stream.start()

    raw[...] = jnp.zeros(raw.shape, raw.dtype)
    raw[pl.ds(c, 1), 0:BLK, 0:BLK] = weight[...][None]

    barrier = pltpu.get_barrier_semaphore()

    def greet(to):
        pl.semaphore_signal(barrier, inc=1, device_id=to, device_id_type=MESH)

    def source_of(i):
        return device(i % 8, 2 * (i // 8) + c, mine, 1 - yl)

    def target_of(i):
        ty, tz = 2 * ((yh + i // 8) % 4) + 1 - c, (z + i) % 8
        return device((z + 64 - 2 * ty - 3 * tz) % 8, ty, tz, yl)

    def peer_row(i):
        other = (pair + i) % 16
        return (dp, 2 * other + c), other

    def peer_col(i):
        other = (dp + i) % 32
        return (other, mp), other

    greet(sibling)
    lax.fori_loop(0, 32, lambda i, _: (greet(source_of(i)), 0)[1], 0)
    for sx, sy, sz, _ in STEPS:
        greet(step_from(x, y, z, c, sx, sy, sz))
    for sx, sy, sz, _, _ in FAR:
        greet(step_from(x, y, z, c, sx, sy, sz))
    lax.fori_loop(1, 16, lambda i, _: (greet(peer_row(i)[0]), 0)[1], 0)
    lax.fori_loop(1, 32, lambda i, _: (greet(peer_col(i)[0]), 0)[1], 0)
    pl.semaphore_wait(barrier, 1 + 32 + 6 + 4 + 15 + 31)

    copy = send(raw.at[c], raw.at[c], raw_s, raw_r, sibling)
    copy.wait()
    rows72[0:BLK, :] = raw[0, 0:BLK, :].astype(jnp.float32)
    rows72[BLK : 2 * BLK, :] = raw[1, 0:BLK, :].astype(jnp.float32)
    lane = lax.broadcasted_iota(jnp.int32, (24, 128), 1)
    together = rows72[0:24, :]
    for g in (1, 2):
        piece = shift_lanes(rows72[24 * g : 24 * g + 24, :], BLK * g)
        together = jnp.where((lane >= BLK * g) & (lane < BLK * g + BLK), piece, together)
    packed[...] = together.astype(jnp.bfloat16)

    def first(i, _):
        send(packed, arrived.at[dp], one_s, one_r, target_of(i))
        return 0

    lax.fori_loop(0, 32, first, 0)

    texts[pl.ds(dp, 1)] = text[...][None]

    def second(i, _):
        to, _ = peer_col(i)
        send(text, texts.at[dp], text_s, text_r, to)
        return 0

    lax.fori_loop(1, 32, second, 0)

    count0, count1, count2 = lengths[0, 0], lengths[0, 1], lengths[0, 2]

    def segment(shape, dim):
        at = lax.broadcasted_iota(jnp.int32, shape, dim)
        return (at >= count0).astype(jnp.int32) + (at >= count0 + count1).astype(jnp.int32)

    same = segment((ROWS, ROWS), 0) == segment((ROWS, ROWS), 1)
    load_qkv.wait()
    root = 1.0 / math.sqrt(HEAD)
    context[...] = jnp.zeros(context.shape, context.dtype)
    for h in range(HEADS):
        q = qkv[:, HEAD * h : HEAD * (h + 1)]
        k = qkv[:, D + HEAD * h : D + HEAD * (h + 1)]
        v = qkv[:, 2 * D + HEAD * h : 2 * D + HEAD * (h + 1)]
        scores = jnp.where(same, dot32(q, k, ((1,), (1,))) * root, jnp.float32(-1e30))
        raised = jnp.exp(scores - jnp.max(scores, axis=1, keepdims=True))
        total = jnp.sum(raised, axis=1, keepdims=True)
        attention = (raised / total).astype(jnp.bfloat16)
        mixed = dot32(attention, v, ((1,), (0,)))
        context[:, SLAB * h : SLAB * h + HEAD] = mixed.astype(jnp.bfloat16)

    await_bytes(arrived, one_r)
    lane = lax.broadcasted_iota(jnp.int32, (24, 128), 1)
    bands = []
    for g in range(3):
        tiles = [None] * 9
        for d in range(32):
            piece = shift_lanes(arrived[d].astype(jnp.float32), BLK * d - BLK * g)
            for t in range(BLK * d // 128, (BLK * d + BLK - 1) // 128 + 1):
                at = lane + 128 * t
                keep = at >= BLK * d
                tiles[t] = piece if tiles[t] is None else jnp.where(keep, piece, tiles[t])
        bands.append(jnp.concatenate(tiles, axis=1))
    bands.append(jnp.zeros((8, D), jnp.float32))
    own = 2 * mine + c
    slabs[pl.ds(own, 1)] = jnp.concatenate(bands, axis=0).astype(jnp.bfloat16)[None]

    copies = []
    for i, (sx, sy, sz, _) in enumerate(STEPS):
        to = step_from(x, y, z, c, sx, sy, sz)
        copies.append(send(slabs.at[own], slabs.at[own], two_s.at[i], two_r.at[i], to))
    for i, (sx, sy, sz, start, size) in enumerate(FAR):
        to = step_from(x, y, z, c, sx, sy, sz)
        part = slabs.at[own, :, pl.ds(start, size)]
        copies.append(send(part, part, two_s.at[6 + i], two_r.at[6 + i], to))
    forwards = [send(slabs.at[own], slabs.at[own], fwd_s.at[0], fwd_r.at[0], sibling)]
    for i, (_, _, _, label) in enumerate(STEPS):
        copies[i].wait_recv()
        at = 2 * ((mine - label + 8) % 8) + c
        forwards.append(send(slabs.at[at], slabs.at[at], fwd_s.at[1 + i], fwd_r.at[1 + i], sibling))
    for i in range(6, 10):
        copies[i].wait_recv()
    at = 2 * ((mine + 4) % 8) + c
    forwards.append(send(slabs.at[at], slabs.at[at], fwd_s.at[7], fwd_r.at[7], sibling))
    for copy in forwards:
        copy.wait_recv()

    load_stream.wait()
    numbers = lax.broadcasted_iota(jnp.int32, (8, ROWS), 0)
    member = (segment((8, ROWS), 1) == numbers).astype(jnp.bfloat16)
    row = lax.broadcasted_iota(jnp.int32, (8, 1), 0)
    counts = jnp.where(row == 0, count0, jnp.where(row == 1, count1, count2)).astype(jnp.float32)
    left = context[...]
    pooled = []
    for n in range(3):
        cols = slice(384 * n, 384 * n + 384)
        right = slabs[:, :, cols].reshape(HEADS * SLAB, 384)
        value = dot32(left, right, ((1,), (0,))) + stream[:, cols].astype(jnp.float32)
        value = value.astype(jnp.bfloat16)
        out[:, cols] = value
        pooled.append(dot32(member, value, ((1,), (0,))))
    pooled = jnp.concatenate(pooled, axis=1) / counts
    unit = pooled / jnp.sqrt(jnp.sum(pooled * pooled, axis=1, keepdims=True) + 1e-6)
    images[pl.ds(c, 1), pl.ds(pair, 1)] = unit[0:3][None, None]

    def third(i, _):
        to, _ = peer_row(i)
        send(images.at[c, pair], images.at[c, pair], img_s, img_r, to)
        return 0

    lax.fori_loop(1, 16, third, 0)

    await_bytes(texts.at[pl.ds(0, 31)], text_r)
    table_t[...] = jnp.zeros(table_t.shape, table_t.dtype)
    for b in range(32):
        table_t[4 * b : 4 * b + 3, :] = texts[b].astype(jnp.float32)
    raw_text = table_t[...]
    norm = jnp.sqrt(jnp.sum(raw_text * raw_text, axis=1, keepdims=True) + 1e-6)
    text_unit = raw_text / norm
    table_i[...] = jnp.zeros(table_i.shape, table_i.dtype)

    await_bytes(images.at[c, pl.ds(0, 15)], img_r)
    forward = send(images.at[c], images.at[c], imf_s, imf_r, sibling)
    forward.wait_recv()
    for b in range(32):
        table_i[4 * b : 4 * b + 3, :] = images[b // 16, b % 16]
    image_unit = table_i[...]

    scale, bias = scale_ref[0], bias_ref[0]
    logits = scale * lax.dot_general(
        image_unit, text_unit, (((1,), (1,)), ((), ())), precision=HIGHEST, preferred_element_type=jnp.float32
    ) + bias
    ri = lax.broadcasted_iota(jnp.int32, (128, 128), 0)
    ci = lax.broadcasted_iota(jnp.int32, (128, 128), 1)
    me_row, me_col = 4 * (c * 16 + pair), 4 * dp
    diagonal = ((ri - me_row) == (ci - me_col)) & (ri >= me_row) & (ri < me_row + 4)
    sign = jnp.where(diagonal, jnp.float32(-1.0), jnp.float32(1.0))
    coef = sign / (1.0 + jnp.exp(-sign * logits))
    coef = jnp.where((ri % 4 < 3) & (ci % 4 < 3), scale * coef, jnp.float32(0.0))
    image_part = lax.dot_general(
        coef, text_unit, (((1,), (0,)), ((), ())), precision=HIGHEST, preferred_element_type=jnp.float32
    )
    table_i[...] = image_part
    for b in range(32):
        part_i[b // 16, b % 16] = table_i[4 * b : 4 * b + 3, :]
    swap = send(part_i.at[1 - c], part_x, mix_s, mix_r, sibling)
    text_part = lax.dot_general(
        coef, image_unit, (((0,), (0,)), ((), ())), precision=HIGHEST, preferred_element_type=jnp.float32
    )
    table_t[...] = text_part
    for b in range(32):
        sent_t[b] = table_t[4 * b : 4 * b + 3, :].astype(sent_t.dtype)

    def fourth(i, _):
        to, other = peer_col(i)
        send(sent_t.at[other], got_t.at[i - 1], gt_s, gt_r, to)
        return 0

    lax.fori_loop(1, 32, fourth, 0)

    swap.wait_recv()
    for b in range(16):
        sent_i[b] = (part_i[pl.ds(c, 1), b][0] + part_x[b]).astype(sent_i.dtype)

    def fifth(i, _):
        to, other = peer_row(i)
        send(sent_i.at[other], got_i.at[i - 1], gi_s, gi_r, to)
        return 0

    lax.fori_loop(1, 16, fifth, 0)

    total = part_i[pl.ds(c, 1), pl.ds(pair, 1)][0, 0] + part_x[pl.ds(pair, 1)][0]
    await_bytes(got_i, gi_r)
    for b in range(15):
        total = total + got_i[b].astype(jnp.float32)
    image_grad[...] = total
    total = sent_t[pl.ds(dp, 1)][0].astype(jnp.float32)
    await_bytes(got_t, gt_r)
    for b in range(31):
        total = total + got_t[b].astype(jnp.float32)
    text_grad[...] = total

    await_bytes(arrived, one_s)
    await_bytes(texts.at[pl.ds(0, 31)], text_s)
    for copy in copies + forwards:
        copy.wait_send()
    await_bytes(images.at[0, pl.ds(0, 15)], img_s)
    forward.wait_send()
    swap.wait_send()
    await_bytes(got_i, gi_s)
    await_bytes(got_t, gt_s)


def per_device(stream, query_key_value, lengths, out_weight, text_embed, logit_scale, logit_bias):
    any_space, vmem, smem = (
        pl.BlockSpec(memory_space=pl.ANY),
        pl.BlockSpec(memory_space=pltpu.VMEM),
        pl.BlockSpec(memory_space=pltpu.SMEM),
    )
    f32, bf16 = jnp.float32, jnp.bfloat16
    dma = pltpu.SemaphoreType.DMA
    return pl.pallas_call(
        kernel,
        out_shape=(
            jax.ShapeDtypeStruct((ROWS, D), bf16),
            jax.ShapeDtypeStruct((3, D), f32),
            jax.ShapeDtypeStruct((3, D), f32),
        ),
        in_specs=[smem, smem, smem, vmem, vmem, any_space, any_space],
        out_specs=(vmem, vmem, vmem),
        scratch_shapes=[
            pltpu.VMEM((ROWS, 3 * D), bf16),
            pltpu.VMEM((ROWS, D), bf16),
            pltpu.VMEM((2, 48, 128), bf16),
            pltpu.VMEM((72, 128), f32),
            pltpu.VMEM((24, 128), bf16),
            pltpu.VMEM((32, 24, 128), bf16),
            pltpu.VMEM((HEADS, SLAB, D), bf16),
            pltpu.VMEM((ROWS, HEADS * SLAB), bf16),
            pltpu.VMEM((32, 3, D), bf16),
            pltpu.VMEM((2, 16, 3, D), f32),
            pltpu.VMEM((128, D), f32),
            pltpu.VMEM((128, D), f32),
            pltpu.VMEM((2, 16, 3, D), f32),
            pltpu.VMEM((16, 3, D), f32),
            pltpu.VMEM((16, 3, D), bf16),
            pltpu.VMEM((15, 3, D), bf16),
            pltpu.VMEM((32, 3, D), bf16),
            pltpu.VMEM((31, 3, D), bf16),
            dma((2,)), dma, dma, dma, dma, dma((10,)), dma((10,)), dma((8,)), dma((8,)),
            dma, dma, dma, dma, dma, dma, dma, dma, dma, dma, dma, dma,
        ],
        compiler_params=pltpu.CompilerParams(
            collective_id=0, has_side_effects=True, vmem_limit_bytes=56 << 20
        ),
    )(lengths, logit_scale, logit_bias, out_weight, text_embed, query_key_value, stream)


def solution(mesh):
    both = P(("dp", "mp"), None)
    return jax.shard_map(
        per_device,
        mesh=mesh,
        in_specs=(both, both, both, P("mp", "dp"), both, P(), P()),
        out_specs=(both, both, both),
        check_vma=False,
    )
```

time: 854 us -> 84.4 us (0.10)
  waiting for transfers between devices: 525 us -> 0 us
  matrix products: 142 us -> 0 us
  blocking collectives: 88.7 us -> 0 us
  Pallas kernels: 0 us -> 77.5 us
  starting transfers between devices: 64.6 us -> 0 us
  between operations: 14.9 us -> 1.93 us
    unnamed x3 -> x0, waiting for transfers between devices: 266 us -> none
    ppermute x32 -> x0, waiting for transfers between devices: 179 us -> none  [from_behind(): return lax.ppermute(block, axis, route)]
    dot_general x99 -> x0, matrix products: 138 us -> none  [the longest x32 57.1 us: coefficients(): jnp.dot(row_images, texts.T, precision=lax.Precision.HIGHEST)]
    all_gather x2 -> x0, blocking collectives: 88.7 us -> none  [the longest x1 49.8 us: per_device(): weight_block = lax.all_gather(out_weight, 'mp', axis=0, tiled=True)]
    all_gather x1 -> x0, waiting for transfers between devices: 79.5 us -> none  [per_device(): lax.all_gather(weight_block, 'dp', axis=1, tiled=True)]
    pallas_call x0 -> x1, Pallas kernels: none -> 77.5 us  [per_device(): pl.pallas_call(kernel, out_shape=(jax.ShapeDtypeStruct((ROWS, D), bf16),...]
    ppermute x32 -> x0, starting transfers between devices: 64.6 us -> none  [from_behind(): return lax.ppermute(block, axis, route)]
  transfers between devices with their start and end apart: 34 -> 0, of which waited for: 34 -> 0; matrix products, arithmetic and copies ran while one was open for 6% -> 0% of each run, Pallas kernels for 0% -> 0%
where the time goes in v1:
time: 84.4 us; the launch traced here: 84 us
  Pallas kernels  77.5 us (92%)
  local copies, waits for them, and re-layouts  4.59 us (5%)
  between operations  1.93 us (2%)
    pallas_call x1, Pallas kernels, per_device(): pl.pallas_call(kernel, out_shape=(jax.ShapeDtypeStruct((ROWS, D), bf16),...  77.5 us
    unnamed x3, local copies, waits for them, and re-layouts  4.59 us

profile of v1, /device:TPU:1, one launch (start us, length us, event | category | flops | bytes accessed | tf_op | source)
XLA Modules:
  0.0 84.0 jit_solution(10649994703054233774)
XLA Ops:
  1.9 77.5 %shard_map.94 = (bf16[256,1152]{1,0:T(8,128)(2,1)}, f32[3,1152]{1,0:T(4,128)}, f32[3,1152]{1,0:T(4,128)}) custom-call(s32[1,3]{1,0:T(1,128)} %lengths.1, f32[1]{0:T(128)S(6)} %copy.13.scale_ref, f32[1]{0:T(128)S(6)} %copy.14.bias_ref, bf16[36,36]{1,0:T(8,128)(2,1)} %weight.1, bf16[3,1152]{1,0:T(4,128)(2,1)} %text.1, bf16[256,3456]{1,0:T(8,128)(2,1)} %qkv_hbm.1, ...), custom_call_target="tpu_custom_call" | custom-call | tf_op jit(solution)/shard_map/pallas_call | solution.py:314
  79.4 1.9 %copy.15 = bf16[256,1152]{1,0:T(8,128)(2,1)} copy(bf16[256,1152]{1,0:T(8,128)(2,1)} %get-tuple-element.6) | data formatting | bytes 1179648
  81.3 1.3 %copy.16 = f32[3,1152]{1,0:T(4,128)} copy(f32[3,1152]{1,0:T(4,128)} %get-tuple-element.7) | data formatting | bytes 27648
  82.7 1.3 %copy.17 = f32[3,1152]{1,0:T(4,128)} copy(f32[3,1152]{1,0:T(4,128)} %get-tuple-element.8) | data formatting | bytes 27648

commit v2 on v0

v2 whole, which is shorter than its diff:
```python
import functools
import math

import jax
import jax.numpy as jnp
from jax import lax
from jax.experimental import pallas as pl
from jax.experimental.pallas import tpu as pltpu
from jax.sharding import PartitionSpec as P

MESH = pl.DeviceIdType.MESH
HEADS = 16
HEAD = 72
SLAB = 80
ROWS = 256
D = 1152
BLK = 36
STEPS = ((1, 0, 0, 1), (-1, 0, 0, -1), (0, 1, 0, 2), (0, -1, 0, -2), (0, 0, 1, 3), (0, 0, -1, -3))
FAR = ((0, 2, 0, 0, 256), (0, -2, 0, 256, 256), (1, 0, 1, 512, 384), (-1, 0, -1, 896, 256))


def place():
    dp, mp = lax.axis_index("dp"), lax.axis_index("mp")
    return dp // 4, 2 * (dp % 4) + (mp // 2) % 2, mp // 4, mp % 2


def device(x, y, z, c):
    return (x * 4 + y // 2, z * 4 + (y % 2) * 2 + c)


def step_from(x, y, z, c, sx, sy, sz):
    return device((x + sx + 8) % 8, (y + sy + 8) % 8, (z + sz + 8) % 8, c)


def send(src, dst, send_sem, recv_sem, to):
    copy = pltpu.make_async_remote_copy(
        src_ref=src, dst_ref=dst, send_sem=send_sem, recv_sem=recv_sem, device_id=to, device_id_type=MESH
    )
    copy.start()
    return copy


def await_bytes(ref, sem):
    pltpu.make_async_copy(ref, ref, sem).wait()


def shift_lanes(value, amount):
    amount = amount % 128
    return value if amount == 0 else pltpu.roll(value, amount, 1)


def split(value):
    high = value.astype(jnp.bfloat16)
    low = (value - high.astype(jnp.float32)).astype(jnp.bfloat16)
    return high, low


def dot32(a, b, dims):
    return lax.dot_general(a, b, (dims, ((), ())), preferred_element_type=jnp.float32)


def kernel(
    lengths, scale_ref, bias_ref, weight, text, qkv_hbm, stream_hbm,
    out, image_grad, text_grad,
    qkv, stream, raw, rows72, packed, arrived, slabs, context, product,
    texts, images, table_i, table_t,
    part_i, part_x, sent_i, got_i, sent_t, got_t,
    local_sem, raw_s, raw_r, one_s, one_r, two_s, two_r, fwd_s, fwd_r,
    text_s, text_r, img_s, img_r, imf_s, imf_r, mix_s, mix_r, gi_s, gi_r, gt_s, gt_r,
):
    x, y, z, c = place()
    dp, mp = lax.axis_index("dp"), lax.axis_index("mp")
    yh, yl = y // 2, y % 2
    pair = z * 2 + yl
    sibling = device(x, y, z, 1 - c)
    mine = (x + 2 * y + 3 * z) % 8

    load_qkv = pltpu.make_async_copy(qkv_hbm, qkv, local_sem.at[0])
    load_qkv.start()
    load_stream = pltpu.make_async_copy(stream_hbm, stream, local_sem.at[1])
    load_stream.start()

    raw[...] = jnp.zeros(raw.shape, raw.dtype)
    raw[pl.ds(c, 1), 0:BLK, 0:BLK] = weight[...][None]

    with jax.named_scope("entry"):
        barrier = pltpu.get_barrier_semaphore()

        def greet(to):
            pl.semaphore_signal(barrier, inc=1, device_id=to, device_id_type=MESH)

        def source_of(i):
            return (i, mine * 4 + c * 2 + 1 - yl)

        def target_of(i):
            th, tz = lax.rem(yh + lax.div(i, 8), 4), lax.rem(z + i, 8)
            tx = lax.rem(z + 64 - 4 * th - 2 * (1 - c) - 3 * tz, 8)
            return (tx * 4 + th, tz * 4 + (1 - c) * 2 + yl)

        def peer_row(i):
            other = lax.rem(pair + i, 16)
            return (dp, 2 * other + c), other

        def peer_col(i):
            other = lax.rem(dp + i, 32)
            return (other, mp), other

        lax.fori_loop(0, 32, lambda i, _: (greet(source_of(i)), 0)[1], 0)
        greet(sibling)
        for sx, sy, sz, _ in STEPS:
            greet(step_from(x, y, z, c, sx, sy, sz))
        for sx, sy, sz, _, _ in FAR:
            greet(step_from(x, y, z, c, sx, sy, sz))
        lax.fori_loop(1, 16, lambda i, _: (greet(peer_row(i)[0]), 0)[1], 0)
        lax.fori_loop(1, 32, lambda i, _: (greet(peer_col(i)[0]), 0)[1], 0)
        pl.semaphore_wait(barrier, 1 + 32 + 6 + 4 + 15 + 31)

    with jax.named_scope("pack"):
        copy = send(raw.at[c], raw.at[c], raw_s, raw_r, sibling)
        copy.wait()
        rows72[0:BLK, :] = raw[0, 0:BLK, :].astype(jnp.float32)
        rows72[BLK : 2 * BLK, :] = raw[1, 0:BLK, :].astype(jnp.float32)
        lane = lax.broadcasted_iota(jnp.int32, (24, 128), 1)
        together = rows72[0:24, :]
        for g in (1, 2):
            piece = shift_lanes(rows72[24 * g : 24 * g + 24, :], BLK * g)
            together = jnp.where((lane >= BLK * g) & (lane < BLK * g + BLK), piece, together)
        packed[...] = together.astype(jnp.bfloat16)

    with jax.named_scope("first_start"):
        def first(i, _):
            send(packed, arrived.at[dp], one_s, one_r, target_of(i))
            return 0

        lax.fori_loop(0, 32, first, 0)

    with jax.named_scope("attention"):
        count0, count1, count2 = lengths[0, 0], lengths[0, 1], lengths[0, 2]

        def segment(shape, dim):
            at = lax.broadcasted_iota(jnp.int32, shape, dim)
            return (at >= count0).astype(jnp.int32) + (at >= count0 + count1).astype(jnp.int32)

        same = segment((ROWS, ROWS), 0) == segment((ROWS, ROWS), 1)
        load_qkv.wait()
        root = 1.0 / math.sqrt(HEAD)
        context[...] = jnp.zeros(context.shape, context.dtype)
        for h in range(HEADS):
            q = qkv[:, HEAD * h : HEAD * (h + 1)]
            k = qkv[:, D + HEAD * h : D + HEAD * (h + 1)]
            v = qkv[:, 2 * D + HEAD * h : 2 * D + HEAD * (h + 1)]
            scores = jnp.where(same, dot32(q, k, ((1,), (1,))) * root, jnp.float32(-1e30))
            raised = jnp.exp(scores - jnp.max(scores, axis=1, keepdims=True))
            total = jnp.sum(raised, axis=1, keepdims=True)
            attention = (raised / total).astype(jnp.bfloat16)
            mixed = dot32(attention, v, ((1,), (0,)))
            at = SLAB * (h // 2)
            context[h % 2, :, at : at + HEAD] = mixed.astype(jnp.bfloat16)

    with jax.named_scope("collect"):
        await_bytes(arrived, one_r)
        lane = lax.broadcasted_iota(jnp.int32, (24, 128), 1)
        bands = []
        for g in range(3):
            tiles = [None] * 9
            for d in range(32):
                piece = shift_lanes(arrived[d].astype(jnp.float32), BLK * d - BLK * g)
                for t in range(BLK * d // 128, (BLK * d + BLK - 1) // 128 + 1):
                    at = lane + 128 * t
                    keep = at >= BLK * d
                    tiles[t] = piece if tiles[t] is None else jnp.where(keep, piece, tiles[t])
            bands.append(jnp.concatenate(tiles, axis=1))
        bands.append(jnp.zeros((8, D), jnp.float32))
        slabs[pl.ds(c, 1), pl.ds(mine, 1)] = jnp.concatenate(bands, axis=0).astype(jnp.bfloat16)[None, None]
        own = slabs.at[c, mine]

    with jax.named_scope("swap_slabs"):
        copies = []
        for i, (sx, sy, sz, _) in enumerate(STEPS):
            to = step_from(x, y, z, c, sx, sy, sz)
            copies.append(send(own, own, two_s.at[i], two_r.at[i], to))
        for i, (sx, sy, sz, start, size) in enumerate(FAR):
            to = step_from(x, y, z, c, sx, sy, sz)
            part = slabs.at[c, mine, :, pl.ds(start, size)]
            copies.append(send(part, part, two_s.at[6 + i], two_r.at[6 + i], to))
        forwards = [send(own, own, fwd_s.at[0], fwd_r.at[0], sibling)]

        texts[pl.ds(dp, 1)] = text[...][None]

        def second(i, _):
            to, _ = peer_col(i)
            send(text, texts.at[dp], text_s, text_r, to)
            return 0

        lax.fori_loop(1, 32, second, 0)

        for i, (_, _, _, label) in enumerate(STEPS):
            copies[i].wait_recv()
            come = slabs.at[c, lax.rem(mine - label + 8, 8)]
            forwards.append(send(come, come, fwd_s.at[1 + i], fwd_r.at[1 + i], sibling))
        for i in range(6, 10):
            copies[i].wait_recv()
        come = slabs.at[c, lax.rem(mine + 4, 8)]
        forwards.append(send(come, come, fwd_s.at[7], fwd_r.at[7], sibling))

    with jax.named_scope("project"):
        load_stream.wait()
        numbers = lax.broadcasted_iota(jnp.int32, (8, ROWS), 0)
        member = (segment((8, ROWS), 1) == numbers).astype(jnp.bfloat16)
        row = lax.broadcasted_iota(jnp.int32, (8, 1), 0)
        counts = jnp.where(row == 0, count0, jnp.where(row == 1, count1, count2)).astype(jnp.float32)
        half = context[pl.ds(c, 1)][0]
        for n in range(3):
            cols = slice(384 * n, 384 * n + 384)
            right = slabs[pl.ds(c, 1), :, :, cols].reshape(HEADS // 2 * SLAB, 384)
            product[:, cols] = dot32(half, right, ((1,), (0,))) + stream[:, cols].astype(jnp.float32)
        for copy in forwards:
            copy.wait_recv()
        half = context[pl.ds(1 - c, 1)][0]
        pooled = []
        for n in range(3):
            cols = slice(384 * n, 384 * n + 384)
            right = slabs[pl.ds(1 - c, 1), :, :, cols].reshape(HEADS // 2 * SLAB, 384)
            value = (product[:, cols] + dot32(half, right, ((1,), (0,)))).astype(jnp.bfloat16)
            out[:, cols] = value
            pooled.append(dot32(member, value, ((1,), (0,))))
        pooled = jnp.concatenate(pooled, axis=1) / counts
        unit = pooled / jnp.sqrt(jnp.sum(pooled * pooled, axis=1, keepdims=True) + 1e-6)
        images[pl.ds(c, 1), pl.ds(pair, 1)] = unit[0:3].astype(jnp.bfloat16)[None, None]

    with jax.named_scope("images_start"):
        def third(i, _):
            to, _ = peer_row(i)
            send(images.at[c, pair], images.at[c, pair], img_s, img_r, to)
            return 0

        lax.fori_loop(1, 16, third, 0)

    with jax.named_scope("text_table"):
        await_bytes(texts.at[pl.ds(0, 31)], text_r)
        table_t[...] = jnp.zeros(table_t.shape, table_t.dtype)
        for b in range(32):
            table_t[4 * b : 4 * b + 3, :] = texts[b].astype(jnp.float32)
        raw_text = table_t[...]
        norm = jnp.sqrt(jnp.sum(raw_text * raw_text, axis=1, keepdims=True) + 1e-6)
        text_rows = raw_text.astype(jnp.bfloat16)
        scale, bias = scale_ref[0, 0], bias_ref[0, 0]

        own_image, own_text = unit[0:3], text[...].astype(jnp.float32)
        own_text = own_text / jnp.sqrt(jnp.sum(own_text * own_text, axis=1, keepdims=True) + 1e-6)
        match = scale * jnp.sum(own_image * own_text, axis=1, keepdims=True) + bias
        match = -scale / (1.0 + jnp.exp(match))
        image_grad[...] = match * own_text
        text_grad[...] = match * own_image
        table_i[...] = jnp.zeros(table_i.shape, table_i.dtype)

    with jax.named_scope("images_wait"):
        await_bytes(images.at[c, pl.ds(0, 15)], img_r)
        forward = send(images.at[c], images.at[c], imf_s, imf_r, sibling)
        forward.wait_recv()
        for b in range(32):
            table_i[4 * b : 4 * b + 3, :] = images[b // 16, b % 16].astype(jnp.float32)
        image_rows = table_i[...].astype(jnp.bfloat16)

    with jax.named_scope("coefficients"):
        logits = scale * (dot32(text_rows, image_rows, ((1,), (1,))) / norm) + bias
        ri = lax.broadcasted_iota(jnp.int32, (128, 128), 0)
        ci = lax.broadcasted_iota(jnp.int32, (128, 128), 1)
        me_row, me_col = 4 * dp, 4 * (c * 16 + pair)
        own = ((ri - me_row) == (ci - me_col)) & (ri >= me_row) & (ri < me_row + 4)
        coef = jnp.where(own | (ri % 4 == 3) | (ci % 4 == 3), jnp.float32(0.0), scale / (1.0 + jnp.exp(-logits)))

    with jax.named_scope("text_partials"):
        high, low = split(coef)
        table_t[...] = dot32(high, image_rows, ((1,), (0,))) + dot32(low, image_rows, ((1,), (0,)))
        for b in range(32):
            sent_t[b] = table_t[4 * b : 4 * b + 3, :].astype(sent_t.dtype)

        def fourth(i, _):
            to, other = peer_col(i)
            send(sent_t.at[other], got_t.at[i - 1], gt_s, gt_r, to)
            return 0

        lax.fori_loop(1, 32, fourth, 0)

    with jax.named_scope("image_partials"):
        high, low = split(coef / norm)
        table_i[...] = dot32(high, text_rows, ((0,), (0,))) + dot32(low, text_rows, ((0,), (0,)))
        for b in range(32):
            part_i[b // 16, b % 16] = table_i[4 * b : 4 * b + 3, :]
        swap = send(part_i.at[1 - c], part_x, mix_s, mix_r, sibling)

    with jax.named_scope("core_sum"):
        swap.wait_recv()
        for b in range(16):
            sent_i[b] = (part_i[pl.ds(c, 1), b][0] + part_x[b]).astype(sent_i.dtype)

        def fifth(i, _):
            to, other = peer_row(i)
            send(sent_i.at[other], got_i.at[i - 1], gi_s, gi_r, to)
            return 0

        lax.fori_loop(1, 16, fifth, 0)

    with jax.named_scope("image_total"):
        total = image_grad[...] + part_i[pl.ds(c, 1), pl.ds(pair, 1)][0, 0] + part_x[pl.ds(pair, 1)][0]
        await_bytes(got_i, gi_r)
        for b in range(15):
            total = total + got_i[b].astype(jnp.float32)
        image_grad[...] = total
    with jax.named_scope("text_total"):
        total = text_grad[...] + sent_t[pl.ds(dp, 1)][0].astype(jnp.float32)
        await_bytes(got_t, gt_r)
        for b in range(31):
            total = total + got_t[b].astype(jnp.float32)
        text_grad[...] = total

    with jax.named_scope("drain"):
        await_bytes(arrived, one_s)
        await_bytes(texts.at[pl.ds(0, 31)], text_s)
        for copy in copies + forwards:
            copy.wait_send()
        await_bytes(images.at[0, pl.ds(0, 15)], img_s)
        forward.wait_send()
        swap.wait_send()
        await_bytes(got_i, gi_s)
        await_bytes(got_t, gt_s)


def hand_out(mixed, image_part, text_part, out, image_grad, text_grad):
    out[...] = mixed[...]
    image_grad[...] = image_part[...]
    text_grad[...] = text_part[...]


def per_device(stream, query_key_value, lengths, out_weight, text_embed, logit_scale, logit_bias):
    any_space, vmem, smem = (
        pl.BlockSpec(memory_space=pl.ANY),
        pl.BlockSpec(memory_space=pltpu.VMEM),
        pl.BlockSpec(memory_space=pltpu.SMEM),
    )
    f32, bf16 = jnp.float32, jnp.bfloat16
    dma = pltpu.SemaphoreType.DMA
    results = pl.pallas_call(
        kernel,
        out_shape=(
            jax.ShapeDtypeStruct((ROWS, D), bf16),
            jax.ShapeDtypeStruct((3, D), f32),
            jax.ShapeDtypeStruct((3, D), f32),
        ),
        in_specs=[smem, smem, smem, vmem, vmem, any_space, any_space],
        out_specs=(vmem, vmem, vmem),
        scratch_shapes=[
            pltpu.VMEM((ROWS, 3 * D), bf16),
            pltpu.VMEM((ROWS, D), bf16),
            pltpu.VMEM((2, 48, 128), bf16),
            pltpu.VMEM((72, 128), f32),
            pltpu.VMEM((24, 128), bf16),
            pltpu.VMEM((32, 24, 128), bf16),
            pltpu.VMEM((2, HEADS // 2, SLAB, D), bf16),
            pltpu.VMEM((2, ROWS, HEADS // 2 * SLAB), bf16),
            pltpu.VMEM((ROWS, D), f32),
            pltpu.VMEM((32, 3, D), bf16),
            pltpu.VMEM((2, 16, 3, D), bf16),
            pltpu.VMEM((128, D), f32),
            pltpu.VMEM((128, D), f32),
            pltpu.VMEM((2, 16, 3, D), f32),
            pltpu.VMEM((16, 3, D), f32),
            pltpu.VMEM((16, 3, D), bf16),
            pltpu.VMEM((15, 3, D), bf16),
            pltpu.VMEM((32, 3, D), bf16),
            pltpu.VMEM((31, 3, D), bf16),
            dma((2,)), dma, dma, dma, dma, dma((10,)), dma((10,)), dma((8,)), dma((8,)),
            dma, dma, dma, dma, dma, dma, dma, dma, dma, dma, dma, dma,
        ],
        compiler_params=pltpu.CompilerParams(
            collective_id=0, has_side_effects=True, vmem_limit_bytes=56 << 20
        ),
    )(lengths, logit_scale.reshape(1, 1), logit_bias.reshape(1, 1), out_weight, text_embed, query_key_value, stream)
    return pl.pallas_call(
        hand_out,
        out_shape=tuple(jax.ShapeDtypeStruct(r.shape, r.dtype) for r in results),
        in_specs=[vmem] * 3,
        out_specs=(vmem,) * 3,
        compiler_params=pltpu.CompilerParams(vmem_limit_bytes=56 << 20),
    )(*results)


def solution(mesh):
    both = P(("dp", "mp"), None)
    return jax.shard_map(
        per_device,
        mesh=mesh,
        in_specs=(both, both, both, P("mp", "dp"), both, P(), P()),
        out_specs=(both, both, both),
        check_vma=False,
    )
```

time: 854 us -> 81.4 us (0.10)
  waiting for transfers between devices: 525 us -> 0 us
  matrix products: 142 us -> 0 us
  blocking collectives: 88.7 us -> 0 us
  Pallas kernels: 0 us -> 79.1 us
  starting transfers between devices: 64.6 us -> 0 us
  between operations: 14.9 us -> 1.93 us
  local copies, waits for them, and re-layouts: 11.9 us -> 0 us
    unnamed x3 -> x0, waiting for transfers between devices: 266 us -> none
    ppermute x32 -> x0, waiting for transfers between devices: 179 us -> none  [from_behind(): return lax.ppermute(block, axis, route)]
    dot_general x99 -> x0, matrix products: 138 us -> none  [the longest x32 57.1 us: coefficients(): jnp.dot(row_images, texts.T, precision=lax.Precision.HIGHEST)]
    all_gather x2 -> x0, blocking collectives: 88.7 us -> none  [the longest x1 49.8 us: per_device(): weight_block = lax.all_gather(out_weight, 'mp', axis=0, tiled=True)]
    all_gather x1 -> x0, waiting for transfers between devices: 79.5 us -> none  [per_device(): lax.all_gather(weight_block, 'dp', axis=1, tiled=True)]
    pallas_call x0 -> x2, Pallas kernels: none -> 79.1 us  [the longest x1 77.2 us: per_device(): pl.pallas_call(kernel, out_shape=(jax.ShapeDtypeStruct((ROWS, D), bf16),...]
    ppermute x32 -> x0, starting transfers between devices: 64.6 us -> none  [from_behind(): return lax.ppermute(block, axis, route)]
    unnamed x14 -> x0, local copies, waits for them, and re-layouts: 8.57 us -> none
  transfers between devices with their start and end apart: 34 -> 0, of which waited for: 34 -> 0; matrix products, arithmetic and copies ran while one was open for 6% -> 0% of each run, Pallas kernels for 0% -> 0%
where the time goes in v2:
time: 81.4 us; the launch traced here: 81.1 us
  Pallas kernels  79.1 us (97%)
  between operations  1.93 us (2%)
    pallas_call x1, Pallas kernels, per_device(): pl.pallas_call(kernel, out_shape=(jax.ShapeDtypeStruct((ROWS, D), bf16),...  77.2 us
    pallas_call x1, Pallas kernels, per_device(): pl.pallas_call(hand_out, out_shape=tuple((jax.ShapeDtypeStruct(r.shape, r...  1.95 us

profile of v2, /device:TPU:1, one launch (start us, length us, event | category | flops | bytes accessed | tf_op | source)
XLA Modules:
  0.0 81.1 jit_solution(9022416201642218188)
XLA Ops:
  1.9 77.2 %shard_map.94 = (bf16[256,1152]{1,0:T(8,128)(2,1)}, f32[3,1152]{1,0:T(4,128)}, f32[3,1152]{1,0:T(4,128)}) custom-call(s32[1,3]{1,0:T(1,128)} %lengths.1, f32[1,1]{1,0:T(1,128)} %bitcast.2.scale_ref, f32[1,1]{1,0:T(1,128)} %bitcast.3.bias_ref, bf16[36,36]{1,0:T(8,128)(2,1)} %weight.1, bf16[3,1152]{1,0:T(4,128)(2,1)} %text.1, bf16[256,3456]{1,0:T(8,128)(2,1)} %qkv_hbm.1, ...), custom_call_target="tpu_custom_call" | custom-call | tf_op jit(solution)/shard_map/pallas_call | solution.py:344
  79.1 1.9 %shard_map.95 = (bf16[256,1152]{1,0:T(8,128)(2,1)}, f32[3,1152]{1,0:T(4,128)}, f32[3,1152]{1,0:T(4,128)}) custom-call(bf16[256,1152]{1,0:T(8,128)(2,1)} %get-tuple-element.6.mixed, f32[3,1152]{1,0:T(4,128)} %get-tuple-element.7.image_part, f32[3,1152]{1,0:T(4,128)} %get-tuple-element.8.text_part), custom_call_target="tpu_custom_call" | custom-call | tf_op jit(solution)/shard_map/pallas_call | solution.py:380

commit v3 on v2

--- a/solution.py
+++ b/solution.py
@@ -145,17 +145,21 @@
         load_qkv.wait()
         root = 1.0 / math.sqrt(HEAD)
         context[...] = jnp.zeros(context.shape, context.dtype)
-        for h in range(HEADS):
-            q = qkv[:, HEAD * h : HEAD * (h + 1)]
-            k = qkv[:, D + HEAD * h : D + HEAD * (h + 1)]
-            v = qkv[:, 2 * D + HEAD * h : 2 * D + HEAD * (h + 1)]
-            scores = jnp.where(same, dot32(q, k, ((1,), (1,))) * root, jnp.float32(-1e30))
-            raised = jnp.exp(scores - jnp.max(scores, axis=1, keepdims=True))
-            total = jnp.sum(raised, axis=1, keepdims=True)
-            attention = (raised / total).astype(jnp.bfloat16)
-            mixed = dot32(attention, v, ((1,), (0,)))
-            at = SLAB * (h // 2)
-            context[h % 2, :, at : at + HEAD] = mixed.astype(jnp.bfloat16)
+
+        def attend(heads):
+            for h in heads:
+                q = qkv[:, HEAD * h : HEAD * (h + 1)]
+                k = qkv[:, D + HEAD * h : D + HEAD * (h + 1)]
+                v = qkv[:, 2 * D + HEAD * h : 2 * D + HEAD * (h + 1)]
+                scores = jnp.where(same, dot32(q, k, ((1,), (1,))) * root, jnp.float32(-1e30))
+                raised = jnp.exp(scores - jnp.max(scores, axis=1, keepdims=True))
+                total = jnp.sum(raised, axis=1, keepdims=True)
+                attention = (raised / total).astype(jnp.bfloat16)
+                mixed = dot32(attention, v, ((1,), (0,)))
+                at = SLAB * (h // 2)
+                context[h % 2, :, at : at + HEAD] = mixed.astype(jnp.bfloat16)
+
+        attend(range(HEADS // 2))
 
     with jax.named_scope("collect"):
         await_bytes(arrived, one_r)
@@ -194,6 +198,7 @@
 
         lax.fori_loop(1, 32, second, 0)
 
+        attend(range(HEADS // 2, HEADS))
         for i, (_, _, _, label) in enumerate(STEPS):
             copies[i].wait_recv()
             come = slabs.at[c, lax.rem(mine - label + 8, 8)]
@@ -209,22 +214,27 @@
         member = (segment((8, ROWS), 1) == numbers).astype(jnp.bfloat16)
         row = lax.broadcasted_iota(jnp.int32, (8, 1), 0)
         counts = jnp.where(row == 0, count0, jnp.where(row == 1, count1, count2)).astype(jnp.float32)
-        half = context[pl.ds(c, 1)][0]
+        half, rest = context[pl.ds(c, 1)][0], context[pl.ds(1 - c, 1)][0]
+        pooled = dot32(member, stream[...], ((1,), (0,)))
+
+        def pool(part, at):
+            sums = dot32(member, part, ((1,), (0,)))
+            high = sums.astype(jnp.bfloat16).astype(jnp.float32)
+            both = jnp.concatenate([high, sums - high], axis=0).astype(jnp.bfloat16)
+            pieces = [dot32(both, block(at, n), ((1,), (0,))) for n in range(3)]
+            both = jnp.concatenate(pieces, axis=1)
+            return both[0:8] + both[8:16]
+
+        def block(at, n):
+            return slabs[pl.ds(at, 1), :, :, 384 * n : 384 * n + 384].reshape(HEADS // 2 * SLAB, 384)
+
+        pooled = pooled + pool(half, c)
         for n in range(3):
             cols = slice(384 * n, 384 * n + 384)
-            right = slabs[pl.ds(c, 1), :, :, cols].reshape(HEADS // 2 * SLAB, 384)
-            product[:, cols] = dot32(half, right, ((1,), (0,))) + stream[:, cols].astype(jnp.float32)
+            product[:, cols] = dot32(half, block(c, n), ((1,), (0,))) + stream[:, cols].astype(jnp.float32)
         for copy in forwards:
             copy.wait_recv()
-        half = context[pl.ds(1 - c, 1)][0]
-        pooled = []
-        for n in range(3):
-            cols = slice(384 * n, 384 * n + 384)
-            right = slabs[pl.ds(1 - c, 1), :, :, cols].reshape(HEADS // 2 * SLAB, 384)
-            value = (product[:, cols] + dot32(half, right, ((1,), (0,)))).astype(jnp.bfloat16)
-            out[:, cols] = value
-            pooled.append(dot32(member, value, ((1,), (0,))))
-        pooled = jnp.concatenate(pooled, axis=1) / counts
+        pooled = (pooled + pool(rest, 1 - c)) / counts
         unit = pooled / jnp.sqrt(jnp.sum(pooled * pooled, axis=1, keepdims=True) + 1e-6)
         images[pl.ds(c, 1), pl.ds(pair, 1)] = unit[0:3].astype(jnp.bfloat16)[None, None]
 
@@ -235,6 +245,11 @@
             return 0
 
         lax.fori_loop(1, 16, third, 0)
+
+    with jax.named_scope("stream_out"):
+        for n in range(3):
+            cols = slice(384 * n, 384 * n + 384)
+            out[:, cols] = (product[:, cols] + dot32(rest, block(1 - c, n), ((1,), (0,)))).astype(jnp.bfloat16)
 
     with jax.named_scope("text_table"):
         await_bytes(texts.at[pl.ds(0, 31)], text_r)
@@ -257,10 +272,12 @@
     with jax.named_scope("images_wait"):
         await_bytes(images.at[c, pl.ds(0, 15)], img_r)
         forward = send(images.at[c], images.at[c], imf_s, imf_r, sibling)
+        for b in range(16):
+            table_i[pl.ds(c, 1), 4 * b : 4 * b + 3, :] = images[pl.ds(c, 1), b].astype(jnp.float32)
         forward.wait_recv()
-        for b in range(32):
-            table_i[4 * b : 4 * b + 3, :] = images[b // 16, b % 16].astype(jnp.float32)
-        image_rows = table_i[...].astype(jnp.bfloat16)
+        for b in range(16):
+            table_i[pl.ds(1 - c, 1), 4 * b : 4 * b + 3, :] = images[pl.ds(1 - c, 1), b].astype(jnp.float32)
+        image_rows = table_i[...].reshape(128, D).astype(jnp.bfloat16)
 
     with jax.named_scope("coefficients"):
         logits = scale * (dot32(text_rows, image_rows, ((1,), (1,))) / norm) + bias
@@ -285,9 +302,11 @@
 
     with jax.named_scope("image_partials"):
         high, low = split(coef / norm)
-        table_i[...] = dot32(high, text_rows, ((0,), (0,))) + dot32(low, text_rows, ((0,), (0,)))
+        part = dot32(high, text_rows, ((0,), (0,))) + dot32(low, text_rows, ((0,), (0,)))
+        table_i[...] = part.reshape(2, 64, D)
         for b in range(32):
-            part_i[b // 16, b % 16] = table_i[4 * b : 4 * b + 3, :]
+            k = b % 16
+            part_i[b // 16, k] = table_i[b // 16, 4 * k : 4 * k + 3, :]
         swap = send(part_i.at[1 - c], part_x, mix_s, mix_r, sibling)
 
     with jax.named_scope("core_sum"):
@@ -362,7 +381,7 @@
             pltpu.VMEM((ROWS, D), f32),
             pltpu.VMEM((32, 3, D), bf16),
             pltpu.VMEM((2, 16, 3, D), bf16),
-            pltpu.VMEM((128, D), f32),
+            pltpu.VMEM((2, 64, D), f32),
             pltpu.VMEM((128, D), f32),
             pltpu.VMEM((2, 16, 3, D), f32),
             pltpu.VMEM((16, 3, D), f32),

time: 81.4 us -> 81 us (level)
  no operation moved by 1% of the time
where the time goes in v3:
time: 81 us; the launch traced here: 80.7 us
  Pallas kernels  78.8 us (97%)
  between operations  1.93 us (2%)
    pallas_call x1, Pallas kernels, per_device(): pl.pallas_call(kernel, out_shape=(jax.ShapeDtypeStruct((ROWS, D), bf16),...  76.8 us
    pallas_call x1, Pallas kernels, per_device(): pl.pallas_call(hand_out, out_shape=tuple((jax.ShapeDtypeStruct(r.shape, r...  1.95 us

profile of v3, /device:TPU:1, one launch (start us, length us, event | category | flops | bytes accessed | tf_op | source)
XLA Modules:
  0.0 80.7 jit_solution(13240973849095151548)
XLA Ops:
  1.9 76.8 %shard_map.94 = (bf16[256,1152]{1,0:T(8,128)(2,1)}, f32[3,1152]{1,0:T(4,128)}, f32[3,1152]{1,0:T(4,128)}) custom-call(s32[1,3]{1,0:T(1,128)} %lengths.1, f32[1,1]{1,0:T(1,128)} %bitcast.2.scale_ref, f32[1,1]{1,0:T(1,128)} %bitcast.3.bias_ref, bf16[36,36]{1,0:T(8,128)(2,1)} %weight.1, bf16[3,1152]{1,0:T(4,128)(2,1)} %text.1, bf16[256,3456]{1,0:T(8,128)(2,1)} %qkv_hbm.1, ...), custom_call_target="tpu_custom_call" | custom-call | tf_op jit(solution)/shard_map/pallas_call | solution.py:363
  78.8 1.9 %shard_map.95 = (bf16[256,1152]{1,0:T(8,128)(2,1)}, f32[3,1152]{1,0:T(4,128)}, f32[3,1152]{1,0:T(4,128)}) custom-call(bf16[256,1152]{1,0:T(8,128)(2,1)} %get-tuple-element.6.mixed, f32[3,1152]{1,0:T(4,128)} %get-tuple-element.7.image_part, f32[3,1152]{1,0:T(4,128)} %get-tuple-element.8.text_part), custom_call_target="tpu_custom_call" | custom-call | tf_op jit(solution)/shard_map/pallas_call | solution.py:399

commit v4 on v3

--- a/solution.py
+++ b/solution.py
@@ -90,20 +90,22 @@
             pl.semaphore_signal(barrier, inc=1, device_id=to, device_id_type=MESH)
 
         def source_of(i):
-            return (i, mine * 4 + c * 2 + 1 - yl)
+            return (lax.rem(dp + 14 + i, 32), mine * 4 + c * 2 + 1 - yl)
 
         def target_of(i):
-            th, tz = lax.rem(yh + lax.div(i, 8), 4), lax.rem(z + i, 8)
+            th, tz = lax.rem(yh + 2 + lax.div(i, 8), 4), lax.rem(z + 4 + i, 8)
             tx = lax.rem(z + 64 - 4 * th - 2 * (1 - c) - 3 * tz, 8)
             return (tx * 4 + th, tz * 4 + (1 - c) * 2 + yl)
 
         def peer_row(i):
-            other = lax.rem(pair + i, 16)
-            return (dp, 2 * other + c), other
+            off = 1 + lax.rem(i + 6, 15)
+            other = lax.rem(pair + off, 16)
+            return (dp, 2 * other + c), other, off - 1
 
         def peer_col(i):
-            other = lax.rem(dp + i, 32)
-            return (other, mp), other
+            off = 1 + lax.rem(i + 12, 31)
+            other = lax.rem(dp + off, 32)
+            return (other, mp), other, off - 1
 
         lax.fori_loop(0, 32, lambda i, _: (greet(source_of(i)), 0)[1], 0)
         greet(sibling)
@@ -179,20 +181,20 @@
         own = slabs.at[c, mine]
 
     with jax.named_scope("swap_slabs"):
-        copies = []
+        copies, pieces = [], []
+        for i, (sx, sy, sz, start, size) in enumerate(FAR):
+            to = step_from(x, y, z, c, sx, sy, sz)
+            part = slabs.at[c, mine, :, pl.ds(start, size)]
+            pieces.append(send(part, part, two_s.at[6 + i], two_r.at[6 + i], to))
         for i, (sx, sy, sz, _) in enumerate(STEPS):
             to = step_from(x, y, z, c, sx, sy, sz)
             copies.append(send(own, own, two_s.at[i], two_r.at[i], to))
-        for i, (sx, sy, sz, start, size) in enumerate(FAR):
-            to = step_from(x, y, z, c, sx, sy, sz)
-            part = slabs.at[c, mine, :, pl.ds(start, size)]
-            copies.append(send(part, part, two_s.at[6 + i], two_r.at[6 + i], to))
         forwards = [send(own, own, fwd_s.at[0], fwd_r.at[0], sibling)]
 
         texts[pl.ds(dp, 1)] = text[...][None]
 
         def second(i, _):
-            to, _ = peer_col(i)
+            to, _, _ = peer_col(i)
             send(text, texts.at[dp], text_s, text_r, to)
             return 0
 
@@ -203,8 +205,8 @@
             copies[i].wait_recv()
             come = slabs.at[c, lax.rem(mine - label + 8, 8)]
             forwards.append(send(come, come, fwd_s.at[1 + i], fwd_r.at[1 + i], sibling))
-        for i in range(6, 10):
-            copies[i].wait_recv()
+        for copy in pieces:
+            copy.wait_recv()
         come = slabs.at[c, lax.rem(mine + 4, 8)]
         forwards.append(send(come, come, fwd_s.at[7], fwd_r.at[7], sibling))
 
@@ -240,7 +242,7 @@
 
     with jax.named_scope("images_start"):
         def third(i, _):
-            to, _ = peer_row(i)
+            to, _, _ = peer_row(i)
             send(images.at[c, pair], images.at[c, pair], img_s, img_r, to)
             return 0
 
@@ -294,8 +296,8 @@
             sent_t[b] = table_t[4 * b : 4 * b + 3, :].astype(sent_t.dtype)
 
         def fourth(i, _):
-            to, other = peer_col(i)
-            send(sent_t.at[other], got_t.at[i - 1], gt_s, gt_r, to)
+            to, other, slot = peer_col(i)
+            send(sent_t.at[other], got_t.at[slot], gt_s, gt_r, to)
             return 0
 
         lax.fori_loop(1, 32, fourth, 0)
@@ -315,8 +317,8 @@
             sent_i[b] = (part_i[pl.ds(c, 1), b][0] + part_x[b]).astype(sent_i.dtype)
 
         def fifth(i, _):
-            to, other = peer_row(i)
-            send(sent_i.at[other], got_i.at[i - 1], gi_s, gi_r, to)
+            to, other, slot = peer_row(i)
+            send(sent_i.at[other], got_i.at[slot], gi_s, gi_r, to)
             return 0
 
         lax.fori_loop(1, 16, fifth, 0)
@@ -337,7 +339,7 @@
     with jax.named_scope("drain"):
         await_bytes(arrived, one_s)
         await_bytes(texts.at[pl.ds(0, 31)], text_s)
-        for copy in copies + forwards:
+        for copy in copies + pieces + forwards:
             copy.wait_send()
         await_bytes(images.at[0, pl.ds(0, 15)], img_s)
         forward.wait_send()

time: 81 us -> 81.3 us (level)
  no operation moved by 1% of the time
where the time goes in v4:
time: 81.3 us; the launch traced here: 81.1 us
  Pallas kernels  79.1 us (97%)
  between operations  1.93 us (2%)
    pallas_call x1, Pallas kernels, per_device(): pl.pallas_call(kernel, out_shape=(jax.ShapeDtypeStruct((ROWS, D), bf16),...  77.2 us
    pallas_call x1, Pallas kernels, per_device(): pl.pallas_call(hand_out, out_shape=tuple((jax.ShapeDtypeStruct(r.shape, r...  1.95 us

profile of v4, /device:TPU:1, one launch (start us, length us, event | category | flops | bytes accessed | tf_op | source)
XLA Modules:
  0.0 81.1 jit_solution(14931880483336280990)
XLA Ops:
  1.9 77.2 %shard_map.94 = (bf16[256,1152]{1,0:T(8,128)(2,1)}, f32[3,1152]{1,0:T(4,128)}, f32[3,1152]{1,0:T(4,128)}) custom-call(s32[1,3]{1,0:T(1,128)} %lengths.1, f32[1,1]{1,0:T(1,128)} %bitcast.2.scale_ref, f32[1,1]{1,0:T(1,128)} %bitcast.3.bias_ref, bf16[36,36]{1,0:T(8,128)(2,1)} %weight.1, bf16[3,1152]{1,0:T(4,128)(2,1)} %text.1, bf16[256,3456]{1,0:T(8,128)(2,1)} %qkv_hbm.1, ...), custom_call_target="tpu_custom_call" | custom-call | tf_op jit(solution)/shard_map/pallas_call | solution.py:365
  79.1 1.9 %shard_map.95 = (bf16[256,1152]{1,0:T(8,128)(2,1)}, f32[3,1152]{1,0:T(4,128)}, f32[3,1152]{1,0:T(4,128)}) custom-call(bf16[256,1152]{1,0:T(8,128)(2,1)} %get-tuple-element.6.mixed, f32[3,1152]{1,0:T(4,128)} %get-tuple-element.7.image_part, f32[3,1152]{1,0:T(4,128)} %get-tuple-element.8.text_part), custom_call_target="tpu_custom_call" | custom-call | tf_op jit(solution)/shard_map/pallas_call | solution.py:401
